TPU v7x, 128 devices: a whole 4x4x4 slice. The times are simulated.
128 devices in a mesh: tp: 4 (over y_hi, core), ep: 32 (over x, y_lo, z).
Axes of the slice: x: 4, y: 4 (y_hi: 2, y_lo: 2; y = y_hi * 2 + y_lo), z: 4, core: 2. Of those that a mesh axis runs over, the one named last changes fastest.
Arguments:
- tokens: bfloat16 [1024, 7168], P(('ep', 'tp')), may hold values from -6 to 6
- routes: int32 [1024, 2], P(('ep', 'tp')), may hold values from 0 to 3, all different within a row; in each aligned block of 8 rows (0 to 7, 8 to 15, ...) at most 8 rows name the same one
- gate_weights: float32 [1024, 2], P(('ep', 'tp')), may hold values from 0.1 to 1
- dense_gate: bfloat16 [7168, 2560], P('ep', 'tp'), may hold values from -0.0625 to 0.0625
- dense_up: bfloat16 [7168, 2560], P('ep', 'tp'), may hold values from -0.0625 to 0.0625
- dense_down: bfloat16 [7168, 2560], P('ep', 'tp'), may hold values from -0.125 to 0.125
- expert_gate: bfloat16 [4, 4864, 7168], P('tp', 'ep'), may hold values from -0.0625 to 0.0625
- expert_up: bfloat16 [4, 4864, 7168], P('tp', 'ep'), may hold values from -0.0625 to 0.0625
- expert_down: bfloat16 [4, 4864, 7168], P('tp', 'ep'), may hold values from -0.078125 to 0.078125
Outputs:
- mixed: bfloat16 [1024, 7168], P(('ep', 'tp'))
Inputs may be any that keep to these rules, and one draw needn't show every extreme that they name: `routes`: the 2 experts of a token differ. Among the 8 tokens of one device (aligned blocks of rows) no expert is named more than 8 times, and in every draw some expert is named exactly 8 times in some block; every expert is named by some token.
All inputs are finite; a program needn't handle non-finite values.
Results may differ from a plain program's by a relative error of at most 0.02.
Values may be sent and summed in bfloat16 or wider, within the bound.
A program may use at most 192 MiB of HBM per device.

v0:
```python
import jax
import jax.numpy as jnp
from jax import lax
from jax.sharding import PartitionSpec as P


def add_piece(activations, weight_piece):
    return jnp.dot(activations, weight_piece, preferred_element_type=jnp.float32)


def by_rows(left, right):
    return lax.dot_general(
        left, right, (((1,), (1,)), ((), ())), preferred_element_type=jnp.float32
    )


def per_device(
    tokens,
    routes,
    gate_weights,
    dense_gate,
    dense_up,
    dense_down,
    expert_gate,
    expert_up,
    expert_down,
):
    width = tokens.shape[1]
    local_tokens = tokens.shape[0]
    tp_count = lax.axis_size("tp")
    gathered = lax.all_gather(tokens, "tp", axis=0, tiled=True)

    def add_single(weight_piece):
        return add_piece(gathered, weight_piece)

    gate_vals = add_single(lax.all_gather(dense_gate, "ep", axis=0, tiled=True))
    up_vals = add_single(lax.all_gather(dense_up, "ep", axis=0, tiled=True))
    dense_hidden = (jax.nn.silu(gate_vals) * up_vals).astype(jnp.bfloat16)
    partial_value = by_rows(dense_hidden, lax.all_gather(dense_down, "ep", axis=0, tiled=True))
    dense_out = lax.psum_scatter(
        partial_value.astype(jnp.bfloat16), "tp", scatter_dimension=0, tiled=True
    ).astype(jnp.float32)
    entries = routes.reshape(-1)
    onehot = (entries[:, None] == jnp.arange(tp_count, dtype=jnp.int32)[None, :]).astype(jnp.int32)
    ranks = jnp.sum(jnp.cumsum(onehot, axis=0) * onehot, axis=1) - 1
    targets = (entries * local_tokens + ranks).reshape(local_tokens, 2)
    slot_ids = jnp.arange(tp_count * local_tokens, dtype=jnp.int32)
    placement = jnp.any(targets[None, :, :] == slot_ids[:, None, None], axis=2).astype(jnp.bfloat16)
    outgoing = jnp.dot(placement, tokens, preferred_element_type=jnp.float32).astype(jnp.bfloat16)
    outgoing = outgoing.reshape(tp_count, local_tokens, width)
    arrived = lax.all_to_all(outgoing, "tp", split_axis=0, concat_axis=0, tiled=True)
    arrived = arrived.reshape(-1, width)
    local_gate = expert_gate[0]
    local_up = expert_up[0]
    local_down = expert_down[0]
    piece = lax.all_gather(arrived, "ep", axis=0, tiled=True)
    e_gate = by_rows(piece, local_gate)
    e_up = by_rows(piece, local_up)
    hidden_all = (jax.nn.silu(e_gate) * e_up).astype(jnp.bfloat16)
    summed = lax.psum_scatter(
        jnp.dot(hidden_all, local_down, preferred_element_type=jnp.float32).astype(jnp.bfloat16),
        "ep",
        scatter_dimension=0,
        tiled=True,
    )
    computed = summed.reshape(tp_count, local_tokens, width)
    returned = lax.all_to_all(computed, "tp", split_axis=0, concat_axis=0, tiled=True)
    returned = returned.reshape(tp_count * local_tokens, width)
    first_rows = jnp.take(returned, targets[:, 0], axis=0).astype(jnp.float32)
    second_rows = jnp.take(returned, targets[:, 1], axis=0).astype(jnp.float32)
    routed = gate_weights[:, 0:1] * first_rows + gate_weights[:, 1:2] * second_rows
    return (tokens.astype(jnp.float32) + dense_out + routed).astype(jnp.bfloat16)


def solution(mesh):
    return jax.shard_map(
        per_device,
        mesh=mesh,
        in_specs=(
            P(("ep", "tp"), None),
            P(("ep", "tp"), None),
            P(("ep", "tp"), None),
            P("ep", "tp"),
            P("ep", "tp"),
            P("ep", "tp"),
            P("tp", "ep", None),
            P("tp", "ep", None),
            P("tp", "ep", None),
        ),
        out_specs=P(("ep", "tp"), None),
        check_vma=False,
    )
```

profile of v0, /device:TPU:1, one launch (start us, length us, event | category | flops | bytes accessed | tf_op | source)
XLA Modules:
  0.0 953.2 jit_solution(4568433679559435468)
XLA Ops:
  6.5 0.0 copy-start
  6.5 0.0 all-gather.11.cloned.1.call-start
  6.5 0.9 copy.14
  7.4 0.1 eq.28
  7.5 0.1 fusion.27
  7.6 0.2 select_reduce_fusion
  7.8 0.1 sub.6
  7.9 0.1 copy.16
  8.0 0.1 fusion.28
  8.1 1.2 fusion
  9.3 14.8 %all_to_all.10 = bf16[4,8,7168]{2,1,0:T(8,128)(2,1)} all-to-all(bf16[4,8,7168]{2,1,0:T(8,128)(2,1)S(1)} %fusion), channel_id=1, replica_groups=mesh['tp'=4,'ep'=32] {'tp'}, dimensions={0} | all-to-all | bytes 917504 | tf_op jit(solution)/shard_map/all_to_all | solution.py:51
  24.1 0.0 all-gather.11.cloned.1.call-update
  24.1 0.0 all-gather.5.cloned.1.call-start
  24.2 0.7 all-gather.5.cloned.1.call-update
  24.9 0.0 all-gather.7.cloned.1.call-start
  24.9 0.7 all-gather.7.cloned.1.call-update
  25.6 0.0 all-gather.9.cloned.1.call-start
  25.6 0.5 all-gather.9.cloned.1.call-update
  26.2 0.0 reduce-scatter.5.cloned.1.call-start
  26.2 166.3 %all-gather.11.cloned.1.call-done = bf16[1024,7168]{1,0:T(8,128)(2,1)} async-done(((bf16[32,7168]{1,0:T(8,128)(2,1)}), bf16[1024,7168]{1,0:T(8,128)(2,1)}) %all-gather.11.cloned.1.call-update) | async-done | bytes 14680080 | tf_op jit(solution)/shard_map/all_gather | solution.py:56
  192.5 10.8 %fusion.4 = f32[1024,152]{0,1:T(8,128)S(1)} fusion(bf16[1024,7168]{1,0:T(8,128)(2,1)} %all-gather.11.cloned.1.call-done, bf16[1,152,7168]{2,1,0:T(8,128)(2,1)} %param.17), kind=kOutput, calls=%fused_computation.9 | convolution fusion | flops 2231369728 | bytes 17481728 | tf_op jit(solution)/shard_map/dot_general | solution.py:12
  203.3 0.0 copy-done
  203.3 22.9 %convolution_convert_fusion = bf16[1024,7168]{1,0:T(8,128)(2,1)} fusion(bf16[1,152,7168]{2,1,0:T(8,128)(2,1)S(1)} %copy-done, bf16[1024,7168]{1,0:T(8,128)(2,1)} %all-gather.11.cloned.1.call-done, bf16[1,152,7168]{2,1,0:T(8,128)(2,1)} %param.18, f32[1024,152]{0,1:T(8,128)S(1)} %fusion.4), kind=kOutput, calls=%fused_computation.2 | convolution fusion | flops 4471013376 | bytes 34340864 | tf_op jit(solution)/shard_map/dot_general | solution.py:61
  226.3 0.0 copy-start.2
  226.3 0.0 reduce-scatter.5.cloned.1.call-update
  226.3 0.0 reduce-scatter.3.cloned.1.call-start
  226.4 0.8 copy-done.2
  227.2 30.4 %all_gather.15 = bf16[32,7168]{1,0:T(8,128)(2,1)S(1)} all-gather(bf16[8,7168]{1,0:T(8,128)(2,1)S(1)} %copy-done.2), channel_id=1, replica_groups=mesh['tp'=4,'ep'=32] {'tp'}, dimensions={0}, use_global_device_ids=true | all-gather | bytes 573440 | tf_op jit(solution)/shard_map/all_gather | solution.py:31
  257.6 99.5 %all-gather.5.cloned.1.call-done = bf16[7168,640]{1,0:T(8,128)(2,1)} async-done(((bf16[224,640]{1,0:T(8,128)(2,1)}), bf16[7168,640]{1,0:T(8,128)(2,1)}) %all-gather.5.cloned.1.call-update) | async-done | bytes 9175056 | tf_op jit(solution)/shard_map/all_gather | solution.py:36
  357.1 0.0 copy-start.1
  357.1 5.3 fusion.31
  362.4 0.0 copy-start.3
  362.4 165.4 %all-gather.7.cloned.1.call-done = bf16[7168,640]{1,0:T(8,128)(2,1)} async-done(((bf16[224,640]{1,0:T(8,128)(2,1)}), bf16[7168,640]{1,0:T(8,128)(2,1)}) %all-gather.7.cloned.1.call-update) | async-done | bytes 9175056 | tf_op jit(solution)/shard_map/all_gather | solution.py:37
  527.8 170.2 %all-gather.9.cloned.1.call-done = bf16[7168,640]{1,0:T(8,128)(2,1)} async-done(((bf16[224,640]{1,0:T(8,128)(2,1)}), bf16[7168,640]{1,0:T(8,128)(2,1)}) %all-gather.9.cloned.1.call-update) | async-done | bytes 9175056 | tf_op jit(solution)/shard_map/all_gather | solution.py:39
  698.0 11.2 %convolution_convert_fusion.2 = bf16[32,7168]{1,0:T(8,128)(2,1)} fusion(bf16[7168,640]{1,0:T(8,128)(2,1)} %all-gather.9.cloned.1.call-done, bf16[32,7168]{1,0:T(8,128)(2,1)S(1)} %all_gather.15, bf16[7168,640]{1,0:T(8,128)(2,1)} %all-gather.7.cloned.1.call-done, f32[32,640]{1,0:T(8,128)S(1)} %fusion.31), kind=kOutput, calls=%fused_computation.4 | convolution fusion | flops 587554816 | bytes 19349504 | tf_op jit(solution)/shard_map/dot_general | solution.py:12
  709.2 0.0 reduce-scatter.3.cloned.1.call-update
  709.3 0.2 slice_reduce_fusion.1
  709.5 187.1 %reduce-scatter.5.cloned.1.call-done = bf16[32,7168]{1,0:T(8,128)(2,1)} async-done(((bf16[1024,7168]{1,0:T(8,128)(2,1)}), bf16[32,7168]{1,0:T(8,128)(2,1)}) %reduce-scatter.5.cloned.1.call-update) | async-done | bytes 458768 | tf_op jit(solution)/shard_map/reduce_scatter | solution.py:60
  896.5 23.8 %all-to-all-start.1 = ((bf16[4,8,7168]{2,1,0:T(8,128)(2,1)}), bf16[4,8,7168]{2,1,0:T(8,128)(2,1)S(1)}, u32[]{:S(2)}, u32[]{:S(2)}) async-start(bf16[4,8,7168]{2,1,0:T(8,128)(2,1)} %bitcast.36), calls=%async_computation.3 | async-start | bytes 917504 | tf_op jit(solution)/shard_map/all_to_all | solution.py:67
  920.4 0.0 copy-done.3
  920.4 8.7 all-to-all-done.1
  929.1 0.6 gather_fusion
  929.7 0.6 gather_fusion.1
  930.4 14.3 %reduce-scatter.3.cloned.1.call-done = bf16[8,7168]{1,0:T(8,128)(2,1)} async-done(((bf16[32,7168]{1,0:T(8,128)(2,1)}), bf16[8,7168]{1,0:T(8,128)(2,1)}) %reduce-scatter.3.cloned.1.call-update) | async-done | bytes 114704 | tf_op jit(solution)/shard_map/reduce_scatter | solution.py:40
  944.7 1.7 add_convert_fusion
  946.4 0.0 copy-done.1
  (8 shorter events, 0.1 us)
Async XLA Ops:
  6.5 196.8 %copy-start = (bf16[1,152,7168]{2,1,0:T(8,128)(2,1)S(1)}, bf16[1,152,7168]{2,1,0:T(8,128)(2,1)}, u32[]{:S(2)}) copy-start(bf16[1,152,7168]{2,1,0:T(8,128)(2,1)} %param.19) | copy-start | bytes 6537220
  6.5 186.0 %all-gather.11.cloned.1.call-start = ((), (), s32[]{:S(2)}) async-start(), calls=%async_computation.8 | async-start | bytes 15138816 | tf_op jit(solution)/shard_map/all_gather | solution.py:56
  24.1 333.0 %all-gather.5.cloned.1.call-start = ((), (), s32[]{:S(2)}) async-start(), calls=%async_computation.4 | async-start | bytes 9461760 | tf_op jit(solution)/shard_map/all_gather | solution.py:36
  24.9 502.9 %all-gather.7.cloned.1.call-start = ((), (), s32[]{:S(2)}) async-start(), calls=%async_computation.5 | async-start | bytes 9461760 | tf_op jit(solution)/shard_map/all_gather | solution.py:37
  25.6 672.4 %all-gather.9.cloned.1.call-start = ((), (), s32[]{:S(2)}) async-start(), calls=%async_computation.6 | async-start | bytes 9461760 | tf_op jit(solution)/shard_map/all_gather | solution.py:39
  26.2 870.4 %reduce-scatter.5.cloned.1.call-start = ((), (), s32[]{:S(2)}) async-start(), calls=%async_computation.9 | async-start | bytes 15138816 | tf_op jit(solution)/shard_map/reduce_scatter | solution.py:60
  226.3 0.9 copy-start.2
  226.3 718.4 %reduce-scatter.3.cloned.1.call-start = ((), (), s32[]{:S(2)}) async-start(), calls=%async_computation.7 | async-start | bytes 573440 | tf_op jit(solution)/shard_map/reduce_scatter | solution.py:40
  357.1 589.2 %copy-start.1 = (bf16[1,152,7168]{2,1,0:T(8,128)(2,1)S(1)}, bf16[1,152,7168]{2,1,0:T(8,128)(2,1)}, u32[]{:S(2)}) copy-start(bf16[1,152,7168]{2,1,0:T(8,128)(2,1)} %param.19) | copy-start | bytes 6537220
  362.4 558.0 %copy-start.3 = (f32[8,2]{0,1:T(2,128)S(1)}, f32[8,2]{0,1:T(2,128)}, u32[]{:S(2)}) copy-start(f32[8,2]{0,1:T(2,128)} %param.13) | copy-start | bytes 196
  896.5 32.6 %all-to-all-start.1 = ((bf16[4,8,7168]{2,1,0:T(8,128)(2,1)}), bf16[4,8,7168]{2,1,0:T(8,128)(2,1)S(1)}, u32[]{:S(2)}, u32[]{:S(2)}) async-start(bf16[4,8,7168]{2,1,0:T(8,128)(2,1)} %bitcast.36), calls=%async_computation.3 | async-start | bytes 917504 | tf_op jit(solution)/shard_map/all_to_all | solution.py:67
Sparse Core Ops, SparseCore 0:
  24.2 168.2 all-gather.10
  194.2 162.8 all-gather.4
  358.8 168.9 all-gather.6
  529.3 168.6 all-gather.8
  700.3 196.2 reduce-scatter.4
  899.0 45.6 reduce-scatter.2
where the time goes:
time: 954 us; the launch traced here: 953 us
  waiting for transfers between devices  814 us (85%)
  matrix products  51.4 us (5%)
  blocking collectives  45.2 us (5%)
  starting transfers between devices  24 us (3%)
  between operations  13.6 us (1%)
    reduce_scatter x1, waiting for transfers between devices, per_device(): lax.psum_scatter(jnp.dot(hidden_all, local_down, preferred_element_type=j...  187 us
    all_gather x1, waiting for transfers between devices, per_device(): lax.all_gather(dense_down, 'ep', axis=0, tiled=True)  170 us
    all_gather x1, waiting for transfers between devices, per_device(): piece = lax.all_gather(arrived, 'ep', axis=0, tiled=True)  166 us
    all_gather x1, waiting for transfers between devices, per_device(): up_vals = add_single(lax.all_gather(dense_up, 'ep', axis=0, tiled=True))  165 us
    all_gather x1, waiting for transfers between devices, per_device(): gate_vals = add_single(lax.all_gather(dense_gate, 'ep', axis=0, tiled=True))  99.5 us
    all_gather x1, blocking collectives, per_device(): gathered = lax.all_gather(tokens, 'tp', axis=0, tiled=True)  30.4 us
    all_to_all x1, starting transfers between devices, per_device(): lax.all_to_all(computed, 'tp', split_axis=0, concat_axis=0, tiled=True)  23.8 us
    dot_general x1, matrix products, per_device(): jnp.dot(hidden_all, local_down, preferred_element_type=jnp.float32)  22.9 us
  transfers between devices with their start and end apart: 7, of which 7 were waited for; matrix products, arithmetic and copies ran while one was open for 5% of the time, Pallas kernels for 0%

commit v1 on v0

v1 whole, which is shorter than its diff:
```python
import jax
import jax.numpy as jnp
from jax import lax
from jax.experimental import pallas as pl
from jax.experimental.pallas import tpu as pltpu
from jax.sharding import PartitionSpec as P

MESH = pl.DeviceIdType.MESH
BF = jnp.bfloat16
F32 = jnp.float32

WIDTH = 7168
HALF = WIDTH // 2
ROWS = 16
UNITS = 192
DENSE_ROWS = 32
EXPERT_ROWS = 152
OUT_COLS = (1280, 1152, 1152)
OFFSET = (0, 1280, 2432)
IN_COLS = (1280, 1152, 1280)
CUT = 640
ORDER = (("y", "x", "z"), ("z", "y", "x"), ("x", "z", "y"))
PARTS = range(3)


def kernel(
    tokens,
    routes,
    weights,
    dense,
    expert_gate,
    expert_up,
    expert_down,
    out,
    x0, x1, x2,
    o0, o1, o2,
    r0, r1, r2,
    *rest,
):
    xs, os, rs = (x0, x1, x2), (o0, o1, o2), (r0, r1, r2)
    rel = [[rest[k * 12 + p * 4:k * 12 + p * 4 + 4] for p in PARTS] for k in range(3)]
    rest = rest[36:]
    (raw, wg, wu, wd, ga, ua, hid, tok_out, tok_in, fin_out, fin_in,
     w_sem, ag_s, ag_r, sib_s, sib_r, rs_s, rs_r, sum_s, sum_r, end_s, end_r) = rest

    ep, tp = lax.axis_index("ep"), lax.axis_index("tp")
    core = lax.rem(tp, 2)
    other = 1 - core
    pos = {
        "x": lax.div(ep, 8),
        "y": lax.div(tp, 2) * 2 + lax.rem(lax.div(ep, 4), 2),
        "z": lax.rem(ep, 4),
    }

    def device(x, y, z, c):
        return {"ep": x * 8 + lax.rem(y, 2) * 4 + z, "tp": lax.div(y, 2) * 2 + c}

    def moved(axis, by):
        place = dict(pos)
        place[axis] = lax.rem(pos[axis] + by, 4)
        return device(place["x"], place["y"], place["z"], core)

    right = {a: moved(a, 1) for a in "xyz"}
    left = {a: moved(a, 3) for a in "xyz"}
    sibling = {"ep": ep, "tp": lax.div(tp, 2) * 2 + other}

    raws = [expert_gate, expert_up, expert_down]
    loads = []
    for n, w in enumerate((wg, wu, wd)):
        loads.append(pltpu.make_async_copy(raws[n].at[0], raw.at[n], w_sem.at[n]))
        for h in range(2):
            loads.append(pltpu.make_async_copy(
                dense.at[n, :, pl.ds(h * HALF, HALF)], w.at[h, pl.ds(0, DENSE_ROWS)], w_sem.at[3 + 2 * n + h]))
    for load in loads:
        load.start()

    barrier = pltpu.get_barrier_semaphore()
    for a in "xyz":
        pl.semaphore_signal(barrier, inc=1, device_id=right[a], device_id_type=MESH)
        pl.semaphore_signal(barrier, inc=1, device_id=left[a], device_id_type=MESH)
    pl.semaphore_signal(barrier, inc=1, device_id=sibling, device_id_type=MESH)
    pl.semaphore_wait(barrier, 7)

    pending = []

    def send(src, dst, s_sem, r_sem, to):
        copy = pltpu.make_async_remote_copy(
            src_ref=src, dst_ref=dst, send_sem=s_sem, recv_sem=r_sem, device_id=to, device_id_type=MESH)
        copy.start()
        pending.append(copy)
        return copy

    lane = lax.broadcasted_iota(jnp.int32, (8, 128), 1)
    named = lax.div(lane, 2)
    factor = jnp.where(routes[:, 0:1] == named, weights[:, 0:1], 0.0) + jnp.where(
        routes[:, 1:2] == named, weights[:, 1:2], 0.0)
    high = factor.astype(BF).astype(F32)
    factor = jnp.where(lax.rem(lane, 2) == 0, high, factor - high)
    tok_out[:, pl.ds(0, HALF)] = tokens[:, pl.ds(pl.multiple_of(other * HALF, 128), HALF)].astype(F32)
    tok_out[:, pl.ds(HALF, 128)] = factor
    swap = send(tok_out, tok_in, end_s.at[0], end_r.at[0], sibling)
    coords = [[pos[a] for a in ORDER[p]] for p in PARTS]
    swap.wait_recv()
    for p in PARTS:
        i1, i2, i3 = coords[p]
        mine = tokens[:, pl.ds(pl.multiple_of(core * HALF + OFFSET[p], 128), OUT_COLS[p])].astype(F32)
        if IN_COLS[p] > OUT_COLS[p]:
            mine = jnp.concatenate([mine, factor], axis=1)
        theirs = tok_in[:, pl.ds(OFFSET[p], IN_COLS[p])]
        first = jnp.where(core == 0, mine, theirs)
        second = jnp.where(core == 0, theirs, mine)
        xs[p][core, i3, i2, i1] = jnp.concatenate([first, second], axis=0).astype(BF)

    def block(p, k, value):
        i1, i2, i3 = coords[p]
        if k == 0:
            return xs[p].at[core, i3, i2, value]
        if k == 1:
            return xs[p].at[core, i3, value]
        return xs[p].at[core, value]

    def half(ref, k, part, cols):
        if k == 0:
            return ref.at[:, pl.ds(0, CUT)] if part == 0 else ref.at[:, pl.ds(CUT, cols - CUT)]
        return ref.at[pl.ds(2 * part, 2)]

    def ring(p, k):
        axis = ORDER[p][k]
        me = pos[axis]
        return axis, me, lax.rem(me + 1, 4), lax.rem(me + 3, 4), lax.rem(me + 2, 4)

    A, B = 0, 1
    flights = {}

    def launch(p, k):
        axis, me, _, _, _ = ring(p, k)
        own = block(p, k, me)
        for part, to, slot in ((A, right, 0), (B, left, 3), (B, right, 1), (A, left, 2)):
            piece = half(own, k, part, IN_COLS[p])
            flights[p, k, slot] = send(piece, piece, ag_s.at[p, k, slot], ag_r.at[p, k, slot], to[axis])

    def relay(p, k):
        axis, me, plus, minus, _ = ring(p, k)
        flights[p, k, 0].wait_recv()
        piece = half(block(p, k, minus), k, A, IN_COLS[p])
        flights[p, k, 4] = send(piece, piece, ag_s.at[p, k, 4], ag_r.at[p, k, 4], right[axis])
        flights[p, k, 3].wait_recv()
        piece = half(block(p, k, plus), k, B, IN_COLS[p])
        flights[p, k, 5] = send(piece, piece, ag_s.at[p, k, 5], ag_r.at[p, k, 5], left[axis])

    shares = {}

    def share(p, n, ref):
        shares[p, n] = send(ref, ref, sib_s.at[p, n], sib_r.at[p, n], sibling)

    def gate_up(p, value, h):
        cols = OUT_COLS[p]
        rows = xs[p][h, value, :, :, :, pl.ds(0, cols)].reshape(256, cols)
        for w, acc in ((wg, ga), (wu, ua)):
            piece = lax.dot_general(
                rows, w[h, :, pl.ds(OFFSET[p], cols)], (((1,), (1,)), ((), ())), preferred_element_type=F32)
            for i in range(4):
                for j in range(4):
                    at = where(p, value, i, j)
                    n = (i * 4 + j) * ROWS
                    acc[at] += piece[n:n + ROWS]

    def where(p, value, second, first):
        place = dict(zip(ORDER[p], (first, second, value)))
        return place["y"], place["z"], place["x"]

    for k in range(2):
        for p in PARTS:
            launch(p, k)
        if k == 1:
            for load in loads:
                load.wait()
            for n, w in enumerate((wg, wu, wd)):
                for h in range(2):
                    w[h, pl.ds(176, 16)] = jnp.zeros((16, HALF), BF)
                    w[h, pl.ds(DENSE_ROWS, EXPERT_ROWS)] = raw[n, :, pl.ds(h * HALF, HALF)]
            ga[...] = jnp.zeros_like(ga)
            ua[...] = jnp.zeros_like(ua)
        for p in PARTS:
            relay(p, k)
        for p in PARTS:
            for slot in (1, 2, 4, 5):
                flights[p, k, slot].wait_recv()

    k = 2
    for p in PARTS:
        launch(p, k)
        share(p, 0, block(p, k, ring(p, k)[1]))
    for p in PARTS:
        gate_up(p, ring(p, k)[1], core)
    for p in PARTS:
        relay(p, k)
        axis, me, plus, minus, _ = ring(p, k)
        share(p, 1, half(block(p, k, minus), k, A, IN_COLS[p]))
        share(p, 2, half(block(p, k, plus), k, B, IN_COLS[p]))
    for p in PARTS:
        shares[p, 0].wait_recv()
        gate_up(p, ring(p, k)[1], other)
    for p in PARTS:
        axis, me, plus, minus, _ = ring(p, k)
        flights[p, k, 1].wait_recv()
        share(p, 3, half(block(p, k, minus), k, B, IN_COLS[p]))
        flights[p, k, 2].wait_recv()
        share(p, 4, half(block(p, k, plus), k, A, IN_COLS[p]))
        gate_up(p, minus, core)
        gate_up(p, plus, core)
    for p in PARTS:
        axis, me, plus, minus, _ = ring(p, k)
        shares[p, 1].wait_recv()
        shares[p, 3].wait_recv()
        gate_up(p, minus, other)
        shares[p, 2].wait_recv()
        shares[p, 4].wait_recv()
        gate_up(p, plus, other)
    for p in PARTS:
        opposite = ring(p, k)[4]
        flights[p, k, 4].wait_recv()
        share(p, 5, half(block(p, k, opposite), k, A, IN_COLS[p]))
        flights[p, k, 5].wait_recv()
        share(p, 6, half(block(p, k, opposite), k, B, IN_COLS[p]))
        gate_up(p, opposite, core)
    for p in PARTS:
        shares[p, 5].wait_recv()
        shares[p, 6].wait_recv()
        gate_up(p, ring(p, k)[4], other)

    lanes = lax.broadcasted_iota(jnp.int32, (256, 128), 1)
    column = lax.broadcasted_iota(jnp.int32, (256, UNITS), 1)
    for y in range(4):
        sent = x2[0, y, :, :, :, pl.ds(OUT_COLS[2], 128)].reshape(256, 128).astype(F32)
        share_of = jnp.sum(jnp.where(lax.div(lanes, 2) == tp, sent, 0.0), axis=1, keepdims=True)
        g = ga[y].reshape(256, UNITS)
        u = ua[y].reshape(256, UNITS)
        value = g / (1.0 + jnp.exp(-g)) * u
        value = value * jnp.where(column < DENSE_ROWS, 1.0, share_of)
        hid[y] = value.astype(BF).reshape(4, 4, ROWS, UNITS)

    for copy in pending:
        copy.wait_send()
    pending.clear()

    def hidden_rows(p, value):
        return jnp.concatenate(
            [hid[where(p, value, i, j)] for i in range(4) for j in range(4)], axis=0)

    def chunks(p):
        return [(c, min(256, OUT_COLS[p] - c)) for c in range(0, OUT_COLS[p], 256)]

    swaps = {}

    def give(p, value, n):
        rows = hidden_rows(p, value)
        for c, size in chunks(p):
            piece = jnp.dot(rows, wd[other, :, pl.ds(OFFSET[p] + c, size)], preferred_element_type=F32)
            xs[p][0, value, :, :, :, pl.ds(c, size)] = piece.astype(BF).reshape(4, 4, ROWS, size)
        swaps[p, n] = send(
            xs[p].at[0, value, :, :, :, pl.ds(0, OUT_COLS[p])], rs[p].at[value], sum_s.at[p, n], sum_r.at[p, n], sibling)

    def keep(p, value, n):
        rows = hidden_rows(p, value)
        swaps[p, n].wait_recv()
        for c, size in chunks(p):
            piece = jnp.dot(rows, wd[core, :, pl.ds(OFFSET[p] + c, size)], preferred_element_type=F32)
            theirs = rs[p][value, :, :, :, pl.ds(c, size)].reshape(256, size).astype(F32)
            os[p][value, :, :, :, pl.ds(c, size)] = (piece + theirs).astype(BF).reshape(4, 4, ROWS, size)

    def add(ref, *more):
        total = ref[...].astype(F32)
        for one in more:
            total = total + one[...].astype(F32)
        ref[...] = total.astype(BF)

    def target(p, k, value):
        i1, i2, i3 = coords[p]
        if k == 2:
            return os[p].at[value]
        if k == 1:
            return os[p].at[i3, value]
        return os[p].at[i3, i2, value]

    sums = {}

    def toss(p, k, slot, src, dst, to):
        sums[p, k, slot] = send(src, dst, rs_s.at[p, k, slot], rs_r.at[p, k, slot], to)

    def first(p, k):
        axis, _, _, _, opposite = ring(p, k)
        rel_a, rel_b, _, _ = rel[k][p]
        cols = OUT_COLS[p]
        blk = target(p, k, opposite)
        toss(p, k, 0, half(blk, k, A, cols), rel_a, right[axis])
        toss(p, k, 1, half(blk, k, B, cols), rel_b, left[axis])

    def to_right_now(p, k):
        axis, _, plus, _, _ = ring(p, k)
        in_left = rel[k][p][2]
        cols = OUT_COLS[p]
        toss(p, k, 2, half(target(p, k, plus), k, B, cols), half(in_left, k, B, cols), right[axis])

    def to_left_now(p, k):
        axis, _, _, minus, _ = ring(p, k)
        in_right = rel[k][p][3]
        cols = OUT_COLS[p]
        toss(p, k, 3, half(target(p, k, minus), k, A, cols), half(in_right, k, A, cols), left[axis])

    def pass_on(p, k):
        axis, _, plus, minus, _ = ring(p, k)
        rel_a, rel_b, in_left, in_right = rel[k][p]
        cols = OUT_COLS[p]
        sums[p, k, 0].wait_recv()
        piece = half(target(p, k, plus), k, A, cols)
        add(piece, rel_a)
        toss(p, k, 4, piece, half(in_left, k, A, cols), right[axis])
        sums[p, k, 1].wait_recv()
        piece = half(target(p, k, minus), k, B, cols)
        add(piece, rel_b)
        toss(p, k, 5, piece, half(in_right, k, B, cols), left[axis])

    def arrived(p, k):
        for slot in (2, 3, 4, 5):
            sums[p, k, slot].wait_recv()

    k = 2
    order = [(p, n) for n in (4, 2, 3, 1) for p in PARTS]
    for step in range(len(order) + 1):
        if step < len(order):
            p, n = order[step]
            give(p, ring(p, k)[n], n)
        if step > 0:
            p, n = order[step - 1]
            keep(p, ring(p, k)[n], n)
            if n == 4:
                first(p, k)
            elif n == 2:
                to_right_now(p, k)
            elif n == 3:
                to_left_now(p, k)
                if p == 2:
                    for q in PARTS:
                        pass_on(q, k)
    for p in PARTS:
        arrived(p, k)
        add(target(p, k, ring(p, k)[1]), rel[k][p][2], rel[k][p][3])
        first(p, 1)
        to_right_now(p, 1)
        to_left_now(p, 1)
    for k in (1, 0):
        for p in PARTS:
            pass_on(p, k)
        for p in PARTS:
            arrived(p, k)
            if k == 1:
                add(target(p, k, ring(p, k)[1]), rel[k][p][2], rel[k][p][3])
                first(p, 0)
                to_right_now(p, 0)
                to_left_now(p, 0)
    here = []
    for p in PARTS:
        total = (target(p, 0, ring(p, 0)[1])[...].astype(F32) + rel[0][p][2][...].astype(F32)
                 + rel[0][p][3][...].astype(F32))
        low, high = total[0:8], total[8:16]
        here.append(jnp.where(core == 0, low, high))
        fin_out[:, pl.ds(OFFSET[p], OUT_COLS[p])] = jnp.where(core == 0, high, low)
    last = send(fin_out, fin_in, end_s.at[1], end_r.at[1], sibling)
    for p in PARTS:
        at = pl.ds(pl.multiple_of(core * HALF + OFFSET[p], 128), OUT_COLS[p])
        out[:, at] = (tokens[:, at].astype(F32) + here[p]).astype(BF)
    last.wait_recv()
    at = pl.ds(pl.multiple_of(other * HALF, 128), HALF)
    out[:, at] = (tokens[:, at].astype(F32) + fin_in[...]).astype(BF)
    for copy in pending:
        copy.wait_send()


def fused(tokens, routes, weights, dense, expert_gate, expert_up, expert_down):
    vmem = pl.BlockSpec(memory_space=pltpu.VMEM)
    hbm = pl.BlockSpec(memory_space=pl.ANY)
    cube = (4, 4, 4, ROWS)
    scratch = [pltpu.VMEM((2, *cube, IN_COLS[p]), BF) for p in PARTS]
    scratch += [pltpu.VMEM((*cube, OUT_COLS[p]), BF) for p in PARTS] * 2
    for k in range(3):
        for p in PARTS:
            cols = OUT_COLS[p]
            if k == 0:
                shapes = [(ROWS, CUT), (ROWS, cols - CUT), (ROWS, cols), (ROWS, cols)]
            elif k == 1:
                shapes = [(2, ROWS, cols)] * 2 + [(4, ROWS, cols)] * 2
            else:
                shapes = [(2, 4, ROWS, cols)] * 2 + [(4, 4, ROWS, cols)] * 2
            scratch += [pltpu.VMEM(s, BF) for s in shapes]
    scratch += [
        pltpu.VMEM((3, EXPERT_ROWS, WIDTH), BF),
        pltpu.VMEM((2, UNITS, HALF), BF),
        pltpu.VMEM((2, UNITS, HALF), BF),
        pltpu.VMEM((2, UNITS, HALF), BF),
        pltpu.VMEM((*cube, UNITS), F32),
        pltpu.VMEM((*cube, UNITS), F32),
        pltpu.VMEM((*cube, UNITS), BF),
        pltpu.VMEM((8, HALF + 128), F32),
        pltpu.VMEM((8, HALF + 128), F32),
        pltpu.VMEM((8, HALF), F32),
        pltpu.VMEM((8, HALF), F32),
        pltpu.SemaphoreType.DMA((9,)),
        pltpu.SemaphoreType.DMA((3, 3, 6)),
        pltpu.SemaphoreType.DMA((3, 3, 6)),
        pltpu.SemaphoreType.DMA((3, 7)),
        pltpu.SemaphoreType.DMA((3, 7)),
        pltpu.SemaphoreType.DMA((3, 3, 6)),
        pltpu.SemaphoreType.DMA((3, 3, 6)),
        pltpu.SemaphoreType.DMA((3, 5)),
        pltpu.SemaphoreType.DMA((3, 5)),
        pltpu.SemaphoreType.DMA((2,)),
        pltpu.SemaphoreType.DMA((2,)),
    ]
    return pl.pallas_call(
        kernel,
        out_shape=jax.ShapeDtypeStruct((8, WIDTH), BF),
        in_specs=[vmem, vmem, vmem, hbm, hbm, hbm, hbm],
        out_specs=vmem,
        scratch_shapes=scratch,
        cost_estimate=pl.CostEstimate(flops=2 * 1024 * 192 * 7168 * 3, bytes_accessed=8_000_000, transcendentals=1024 * 192),
        compiler_params=pltpu.CompilerParams(
            collective_id=0, has_side_effects=True, vmem_limit_bytes=63 * 2**20),
    )(tokens, routes, weights, dense, expert_gate, expert_up, expert_down)


def per_device(tokens, routes, gate_weights, dense_gate, dense_up, dense_down, expert_gate, expert_up, expert_down):
    n = lax.axis_size("ep")

    def own_units(weight):
        rows, units = weight.shape
        return weight.T.reshape(n, units // n, rows)

    packed = jnp.stack([own_units(w) for w in (dense_gate, dense_up, dense_down)], axis=1)
    there = lax.all_to_all(packed, "ep", split_axis=0, concat_axis=0, tiled=True)
    there = there.transpose(1, 2, 0, 3).reshape(3, packed.shape[2], tokens.shape[1])
    dense = jnp.pad(there, ((0, 0), (0, DENSE_ROWS - there.shape[1]), (0, 0)))
    return fused(tokens, routes, gate_weights, dense, expert_gate, expert_up, expert_down)


def solution(mesh):
    return jax.shard_map(
        per_device,
        mesh=mesh,
        in_specs=(
            P(("ep", "tp"), None),
            P(("ep", "tp"), None),
            P(("ep", "tp"), None),
            P("ep", "tp"),
            P("ep", "tp"),
            P("ep", "tp"),
            P("tp", "ep", None),
            P("tp", "ep", None),
            P("tp", "ep", None),
        ),
        out_specs=P(("ep", "tp"), None),
        check_vma=False,
    )
```

time: 954 us -> 132 us (0.14)
  waiting for transfers between devices: 814 us -> 14.7 us
  Pallas kernels: 0 us -> 97 us
  matrix products: 51.4 us -> 0 us
  blocking collectives: 45.2 us -> 0 us
  starting transfers between devices: 24 us -> 9.86 us
  between operations: 13.6 us -> 0.1 us
    all_gather x4 -> x0, waiting for transfers between devices: 601 us -> none  [the longest x1 170 us: per_device(): lax.all_gather(dense_down, 'ep', axis=0, tiled=True)]
    reduce_scatter x2 -> x0, waiting for transfers between devices: 201 us -> none  [the longest x1 187 us: per_device(): lax.psum_scatter(jnp.dot(hidden_all, local_down, preferred_element_type=j...]
    pallas_call x0 -> x1, Pallas kernels: none -> 97 us  [fused(): pl.pallas_call(kernel, out_shape=jax.ShapeDtypeStruct((8, WIDTH), BF), in...]
    dot_general x5 -> x0, matrix products: 51.4 us -> none  [the longest x1 22.9 us: per_device(): jnp.dot(hidden_all, local_down, preferred_element_type=jnp.float32)]
    all_gather x1 -> x0, blocking collectives: 30.4 us -> none  [per_device(): gathered = lax.all_gather(tokens, 'tp', axis=0, tiled=True)]
    all_to_all x1 -> x0, blocking collectives: 14.8 us -> none  [per_device(): lax.all_to_all(outgoing, 'tp', split_axis=0, concat_axis=0, tiled=True)]
    all_to_all x1, starting transfers between devices: 23.8 us -> 9.86 us  [per_device(): lax.all_to_all(packed, 'ep', split_axis=0, concat_axis=0, tiled=True)]
  transfers between devices with their start and end apart: 7 -> 1, of which waited for: 7 -> 1; matrix products, arithmetic and copies ran while one was open for 5% -> 1% of each run, Pallas kernels for 0% -> 0%
where the time goes in v1:
time: 132 us; the launch traced here: 131 us
  Pallas kernels  97 us (73%)
  waiting for transfers between devices  14.7 us (11%)
  starting transfers between devices  9.86 us (7%)
  local copies, waits for them, and re-layouts  9.59 us (7%)
    pallas_call x1, Pallas kernels, fused(): pl.pallas_call(kernel, out_shape=jax.ShapeDtypeStruct((8, WIDTH), BF), in...  97 us
    all_to_all x1, waiting for transfers between devices, per_device(): lax.all_to_all(packed, 'ep', split_axis=0, concat_axis=0, tiled=True)  14.7 us
    all_to_all x1, starting transfers between devices, per_device(): lax.all_to_all(packed, 'ep', split_axis=0, concat_axis=0, tiled=True)  9.86 us
    unnamed x11, local copies, waits for them, and re-layouts  3.48 us
  transfers between devices with their start and end apart: 1, of which 1 were waited for; matrix products, arithmetic and copies ran while one was open for 1% of the time, Pallas kernels for 0%

profile of v1, /device:TPU:1, one launch (start us, length us, event | category | flops | bytes accessed | tf_op | source)
XLA Modules:
  0.0 131.5 jit_solution(16568091956273565190)
XLA Ops:
  0.0 0.0 copy-start
  0.0 1.2 copy.22
  1.2 0.0 copy-start.1
  1.2 0.1 stack_reshape.10
  1.3 0.0 copy-done
  1.3 0.2 copy.23
  1.5 0.1 stack_reshape.11
  1.6 0.6 copy-done.1
  2.1 0.2 copy.21
  2.3 0.1 stack_reshape.9
  2.4 0.3 pad_maximum_fusion
  2.7 1.1 copy.24
  3.8 0.0 copy-start.2
  3.8 0.0 copy-start.3
  3.8 9.9 %all-to-all-start = ((bf16[32,3,20,224]{3,2,1,0:T(8,128)(2,1)}), bf16[32,3,20,224]{3,2,1,0:T(8,128)(2,1)S(1)}, u32[]{:S(2)}, u32[]{:S(2)}) async-start(bf16[32,3,20,224]{3,2,1,0:T(8,128)(2,1)} %copy.24), calls=%async_computation | async-start | bytes 2359296 | tf_op jit(solution)/shard_map/all_to_all | solution.py:440
  13.7 0.0 copy-done.2
  13.7 0.7 copy.26.routes
  14.4 0.0 copy-done.3
  14.4 0.7 copy.27.weights
  15.0 14.7 %all-to-all-done = bf16[32,3,20,224]{3,2,1,0:T(8,128)(2,1)S(1)} async-done(((bf16[32,3,20,224]{3,2,1,0:T(8,128)(2,1)}), bf16[32,3,20,224]{3,2,1,0:T(8,128)(2,1)S(1)}, u32[]{:S(2)}, u32[]{:S(2)}) %all-to-all-start) | async-done | bytes 860192 | tf_op jit(solution)/shard_map/all_to_all | solution.py:440
  29.7 0.2 copy.25
  29.9 1.8 %reshape.3 = bf16[3,20,7168]{2,1,0:T(8,128)(2,1)S(1)} reshape(bf16[3,20,32,224]{3,2,1,0:T(8,128)(2,1)S(1)} %copy.25) | data formatting | bytes 1720320 | tf_op jit(solution)/shard_map/reshape | solution.py:441
  31.7 1.2 pad.4.dense
  33.0 97.0 %shard_map.91 = bf16[8,7168]{1,0:T(8,128)(2,1)} custom-call(bf16[8,7168]{1,0:T(8,128)(2,1)} %tokens.1, s32[8,2]{1,0:T(8,128)} %copy.26.routes, f32[8,2]{1,0:T(8,128)} %copy.27.weights, bf16[3,32,7168]{2,1,0:T(8,128)(2,1)} %pad.4.dense, bf16[1,152,7168]{2,1,0:T(8,128)(2,1)} %expert_gate.1, bf16[1,152,7168]{2,1,0:T(8,128)(2,1)} %expert_up.1, ...), custom_call_target="tpu_custom_call" | custom-call | flops 8455716864 | bytes 8000000 | tf_op jit(solution)/shard_map/pallas_call | solution.py:420
  129.9 1.6 %copy.29 = bf16[8,7168]{1,0:T(8,128)(2,1)} copy(bf16[8,7168]{1,0:T(8,128)(2,1)} %shard_map.91) | data formatting | bytes 229376
Async XLA Ops:
  0.0 1.3 copy-start
  1.2 1.0 copy-start.1
  3.8 9.9 %copy-start.2 = (s32[8,2]{0,1:T(2,128)S(1)}, s32[8,2]{0,1:T(2,128)}, u32[]{:S(2)}) copy-start(s32[8,2]{0,1:T(2,128)} %param.10) | copy-start | bytes 196
  3.8 10.6 %copy-start.3 = (f32[8,2]{0,1:T(2,128)S(1)}, f32[8,2]{0,1:T(2,128)}, u32[]{:S(2)}) copy-start(f32[8,2]{0,1:T(2,128)} %param.11) | copy-start | bytes 196
  3.8 25.9 %all-to-all-start = ((bf16[32,3,20,224]{3,2,1,0:T(8,128)(2,1)}), bf16[32,3,20,224]{3,2,1,0:T(8,128)(2,1)S(1)}, u32[]{:S(2)}, u32[]{:S(2)}) async-start(bf16[32,3,20,224]{3,2,1,0:T(8,128)(2,1)} %copy.24), calls=%async_computation | async-start | bytes 2359296 | tf_op jit(solution)/shard_map/all_to_all | solution.py:440

commit v2 on v0

v2 whole, which is shorter than its diff:
```python
import jax
import jax.numpy as jnp
from jax import lax
from jax.experimental import pallas as pl
from jax.experimental.pallas import tpu as pltpu
from jax.sharding import PartitionSpec as P

MESH = pl.DeviceIdType.MESH
BF = jnp.bfloat16
F32 = jnp.float32

WIDTH = 7168
HALF = WIDTH // 2
ROWS = 16
UNITS = 192
DENSE_ROWS = 32
EXPERT_ROWS = 152
DEPTH = 224
RUN = 4 * DEPTH
OUT_COLS = (1280, 1152, 1152)
OFFSET = (0, 1280, 2432)
IN_COLS = (1280, 1152, 1280)
CUT = 640
ORDER = (("y", "x", "z"), ("z", "y", "x"), ("x", "z", "y"))
PARTS = range(3)
OWN, RIGHT, LEFT, FAR = range(4)
BOTH = pl.ds(1, 2)
OTHERS = pl.ds(1, 3)
LINE = (0, OTHERS)
PLANE = ((0, 0), (0, OTHERS), (OTHERS, 0), (BOTH, OTHERS), (3, OTHERS))
A, B = 0, 1
FLIGHTS = 48


def cut(selected, part, cols):
    if part is None:
        return tuple(selected)
    if selected and selected[0] is BOTH:
        return (1 + part, *selected[1:])
    side = pl.ds(0, CUT) if part == A else pl.ds(CUT, cols - CUT)
    return (*selected, slice(None), side)


def view(ref, index):
    return ref.at[index] if index else ref


def kernel(
    tokens, routes, weights, packed, expert_gate, expert_up, expert_down,
    out,
    x0, x1, x2, o0, o1, o2, r0, r1, r2,
    *rest,
):
    xs, os, rs = (x0, x1, x2), (o0, o1, o2), (r0, r1, r2)
    passing = {(k, p): rest[(k - 1) * 3 + p] for k in (1, 2) for p in PARTS}
    sides = {(k, p): rest[6 + (k - 1) * 3 + p] for k in (1, 2) for p in PARTS}
    threes = {(k, p): rest[12 + k * 3 + p] for k in (0, 1) for p in PARTS}
    rest = rest[18:]
    (raw, wg, wu, wd, ga, ua, hid, tok_out, tok_in, fin_out, fin_in, dbuf,
     w_sem, d_s, d_r, out_s, ag_r, sib_r, rs_r, sum_r, end_r) = rest

    ep, tp = lax.axis_index("ep"), lax.axis_index("tp")
    core = lax.rem(tp, 2)
    other = 1 - core
    pos = {
        "x": lax.div(ep, 8),
        "y": lax.div(tp, 2) * 2 + lax.rem(lax.div(ep, 4), 2),
        "z": lax.rem(ep, 4),
    }

    def device(x, y, z):
        return {"ep": x * 8 + lax.rem(y, 2) * 4 + z, "tp": lax.div(y, 2) * 2 + core}

    def moved(axis, by):
        place = dict(pos)
        place[axis] = lax.rem(pos[axis] + by, 4)
        return device(place["x"], place["y"], place["z"])

    right = {a: moved(a, 1) for a in "xyz"}
    left = {a: moved(a, 3) for a in "xyz"}
    far = {a: moved(a, 2) for a in "xyz"}
    sibling = {"ep": ep, "tp": lax.div(tp, 2) * 2 + other}

    loads = [
        pltpu.make_async_copy(w.at[0], raw.at[n], w_sem.at[n])
        for n, w in enumerate((expert_gate, expert_up, expert_down))
    ]
    loads.append(pltpu.make_async_copy(packed.at[ep], dbuf.at[ep], d_r))
    for load in loads:
        load.start()

    y_low = lax.rem(pos["y"], 2)
    steps = sorted(
        ((dx, dy, dz) for dx in range(4) for dy in range(2) for dz in range(4) if dx or dy or dz),
        key=lambda d: min(d[0], 4 - d[0]) + d[1] + min(d[2], 4 - d[2]))

    def peer(dx, dy, dz):
        return lax.rem(pos["x"] + dx, 4) * 8 + lax.rem(y_low + dy, 2) * 4 + lax.rem(pos["z"] + dz, 4)

    peers = [peer(*d) for d in steps]

    barrier = pltpu.get_barrier_semaphore()
    pl.semaphore_signal(barrier, inc=1, device_id=sibling, device_id_type=MESH)
    for by in (1, 2, 3):
        pl.semaphore_signal(barrier, inc=1, device_id=moved("y", by), device_id_type=MESH)
    for d, to in zip(steps, peers):
        if d != (0, 1, 0):
            pl.semaphore_signal(barrier, inc=1, device_id={"ep": to, "tp": tp}, device_id_type=MESH)
    pl.semaphore_wait(barrier, 34)

    flying = []

    def send(src, dst, r_sem, to):
        n = len(flying)
        if n >= FLIGHTS:
            flying[n - FLIGHTS].wait_send()
        copy = pltpu.make_async_remote_copy(
            src_ref=src, dst_ref=dst, send_sem=out_s.at[n % FLIGHTS], recv_sem=r_sem, device_id=to, device_id_type=MESH)
        copy.start()
        flying.append(copy)
        return copy

    def settle():
        for copy in flying[max(0, len(flying) - FLIGHTS):]:
            copy.wait_send()
        flying.clear()

    def landed(ref, sem):
        pltpu.make_async_copy(ref, ref, sem).wait()

    diagonal = lax.broadcasted_iota(jnp.int32, (8, 8), 0) == lax.broadcasted_iota(jnp.int32, (8, 8), 1)

    def column_of(row):
        return jnp.sum(jnp.where(diagonal, jnp.broadcast_to(row, (8, 8)), jnp.zeros((8, 8), row.dtype)), axis=1, keepdims=True)

    lane = lax.broadcasted_iota(jnp.int32, (8, 128), 1)
    named = lax.div(lane, 2).astype(F32)
    chosen = [column_of(routes[n:n + 1, :].astype(F32)) for n in range(2)]
    factor = jnp.where(chosen[0] == named, column_of(weights[0:1, :]), 0.0) + jnp.where(
        chosen[1] == named, column_of(weights[1:2, :]), 0.0)
    high = factor.astype(BF).astype(F32)
    factor = jnp.where(lax.rem(lane, 2) == 0, high, factor - high)
    tok_out[:, pl.ds(0, HALF)] = tokens[:, pl.ds(pl.multiple_of(other * HALF, 128), HALF)].astype(F32)
    tok_out[:, pl.ds(HALF, 128)] = factor
    swap = send(tok_out, tok_in, end_r.at[0], sibling)
    swap.wait_recv()
    for p in PARTS:
        mine = tokens[:, pl.ds(pl.multiple_of(core * HALF + OFFSET[p], 128), OUT_COLS[p])].astype(F32)
        if IN_COLS[p] > OUT_COLS[p]:
            mine = jnp.concatenate([mine, factor], axis=1)
        theirs = tok_in[:, pl.ds(OFFSET[p], IN_COLS[p])]
        first = jnp.where(core == 0, mine, theirs)
        second = jnp.where(core == 0, theirs, mine)
        xs[p][core, 0, 0, 0] = jnp.concatenate([first, second], axis=0).astype(BF)

    def chunks_of(k):
        return ((),) if k == 0 else tuple((s,) for s in LINE) if k == 1 else PLANE

    def token_view(p, k, place, c, part=None):
        prefix = {0: (core, 0, 0, place), 1: (core, 0, place), 2: (core, place)}[k]
        return xs[p].at[(*prefix, *cut(chunks_of(k)[c], part, IN_COLS[p]))]

    def ag_slot(k, c, n):
        return 0 if k == 0 else (0, 1, 5)[k] + 2 * c + n

    def fly(p, k, c, n, src, dst, to):
        send(src, dst, ag_r.at[p, ag_slot(k, c, n)], to[ORDER[p][k]])

    def spread(p, k, c=0, direct=False):
        own = token_view(p, k, OWN, c)
        fly(p, k, c, 0, own, token_view(p, k, LEFT, c), right)
        fly(p, k, c, 0, own, token_view(p, k, RIGHT, c), left)
        if direct:
            fly(p, k, c, 1, own, token_view(p, k, FAR, c), far)

    def near(p, k, c=0):
        landed(token_view(p, k, OTHERS if k == 0 else BOTH, c), ag_r.at[p, ag_slot(k, c, 0)])

    def relay(p, k, c=0):
        near(p, k, c)
        fly(p, k, c, 1, token_view(p, k, LEFT, c, A), token_view(p, k, FAR, c, A), right)
        fly(p, k, c, 1, token_view(p, k, RIGHT, c, B), token_view(p, k, FAR, c, B), left)

    def distant(p, k, c=0):
        landed(token_view(p, k, FAR, c), ag_r.at[p, ag_slot(k, c, 1)])

    shares = {}

    def share(p, n, ref):
        shares[p, n] = send(ref, ref, sib_r.at[p, n], sibling)

    def where(p, third, second, first):
        place = dict(zip(ORDER[p], (first, second, third)))
        return place["y"], place["z"], place["x"]

    def gate_up(p, place, h):
        cols = OUT_COLS[p]
        rows = xs[p][h, place, :, :, :, pl.ds(0, cols)].reshape(256, cols)
        for w, acc in ((wg, ga), (wu, ua)):
            piece = lax.dot_general(
                rows, w[h, :, pl.ds(OFFSET[p], cols)], (((1,), (1,)), ((), ())), preferred_element_type=F32)
            for i in range(4):
                for j in range(4):
                    n = (i * 4 + j) * ROWS
                    acc[where(p, place, i, j)] += piece[n:n + ROWS]

    def dense_out(first, last):
        for to in peers[first:last]:
            pltpu.make_async_remote_copy(
                src_ref=packed.at[to], dst_ref=dbuf.at[ep], send_sem=d_s, recv_sem=d_r,
                device_id={"ep": to, "tp": tp}, device_id_type=MESH).start()

    def dense_in():
        landed(dbuf, d_r)
        row = lax.broadcasted_iota(jnp.int32, (ROWS, RUN), 0)
        for i in range(8):
            at = pl.ds((i % 4) * RUN, RUN)
            run = jnp.concatenate([dbuf[4 * i + z][:, 0:DEPTH].astype(F32) for z in range(4)], axis=1)
            tail = run[48:64]
            for n, w in enumerate((wg, wu, wd)):
                w[i // 4, pl.ds(0, 16), at] = run[16 * n:16 * n + 16].astype(BF)
                turned = tail if n == 0 else pltpu.roll(tail, 16 - 4 * n, 0)
                w[i // 4, pl.ds(16, 16), at] = jnp.where(row < 4, turned, 0.0).astype(BF)

    def expert_in():
        for load in loads[:3]:
            load.wait()
        for n, w in enumerate((wg, wu, wd)):
            for h in range(2):
                w[h, pl.ds(176, 16)] = jnp.zeros((16, HALF), BF)
                w[h, pl.ds(DENSE_ROWS, EXPERT_ROWS)] = raw[n, :, pl.ds(h * HALF, HALF)]
        ga[...] = jnp.zeros_like(ga)
        ua[...] = jnp.zeros_like(ua)

    for p in PARTS:
        spread(p, 0, direct=True)
    for p in PARTS:
        spread(p, 1, 0, direct=True)
    dense_out(0, 8)
    for p in PARTS:
        spread(p, 2, 0)
    dense_out(8, 16)
    for p in PARTS:
        near(p, 0)
        spread(p, 1, 1)
        spread(p, 2, 1)
    dense_out(16, 24)
    for p in PARTS:
        near(p, 1, 0)
        distant(p, 1, 0)
        spread(p, 2, 2)
    dense_out(24, 31)
    for p in PARTS:
        relay(p, 2, 0)
    for p in PARTS:
        relay(p, 1, 1)
        spread(p, 2, 3)
    for p in PARTS:
        distant(p, 1, 1)
        spread(p, 2, 4)
        share(p, 0, xs[p].at[core, 0])
    expert_in()
    for p in PARTS:
        relay(p, 2, 1)
    for p in PARTS:
        relay(p, 2, 2)
    dense_in()
    for p in PARTS:
        relay(p, 2, 3)
    for p in PARTS:
        gate_up(p, OWN, core)
    for p in PARTS:
        relay(p, 2, 4)
        share(p, 1, xs[p].at[core, RIGHT])
        share(p, 2, xs[p].at[core, LEFT])
    for p in PARTS:
        shares[p, 0].wait_recv()
        gate_up(p, OWN, other)
    for p in PARTS:
        gate_up(p, RIGHT, core)
        gate_up(p, LEFT, core)
    for p in PARTS:
        for c in (0, 1):
            distant(p, 2, c)
        share(p, 3, xs[p].at[core, FAR, 0])
    for p in PARTS:
        shares[p, 1].wait_recv()
        gate_up(p, RIGHT, other)
        shares[p, 2].wait_recv()
        gate_up(p, LEFT, other)
    for p in PARTS:
        for c in (2, 3, 4):
            distant(p, 2, c)
        share(p, 4, xs[p].at[core, FAR, OTHERS])
    for p in PARTS:
        gate_up(p, FAR, core)
    for p in PARTS:
        shares[p, 3].wait_recv()
        shares[p, 4].wait_recv()
        gate_up(p, FAR, other)

    lanes = lax.broadcasted_iota(jnp.int32, (256, 128), 1)
    column = lax.broadcasted_iota(jnp.int32, (256, UNITS), 1)
    for y in range(4):
        sent = x2[0, y, :, :, :, pl.ds(OUT_COLS[2], 128)].reshape(256, 128).astype(F32)
        share_of = jnp.sum(jnp.where(lax.div(lanes, 2) == tp, sent, 0.0), axis=1, keepdims=True)
        g = ga[y].reshape(256, UNITS)
        u = ua[y].reshape(256, UNITS)
        value = g / (1.0 + jnp.exp(-g)) * u
        value = value * jnp.where(column < DENSE_ROWS, 1.0, share_of)
        hid[y] = value.astype(BF).reshape(4, 4, ROWS, UNITS)

    settle()

    def hidden_rows(p, place):
        return jnp.concatenate([hid[where(p, place, i, j)] for i in range(4) for j in range(4)], axis=0)

    def pieces(p):
        return [(c, min(256, OUT_COLS[p] - c)) for c in range(0, OUT_COLS[p], 256)]

    swaps = {}

    def give(p, place):
        rows = hidden_rows(p, place)
        for c, size in pieces(p):
            piece = jnp.dot(rows, wd[other, :, pl.ds(OFFSET[p] + c, size)], preferred_element_type=F32)
            xs[p][0, place, :, :, :, pl.ds(c, size)] = piece.astype(BF).reshape(4, 4, ROWS, size)
        swaps[p, place] = send(
            xs[p].at[0, place, :, :, :, pl.ds(0, OUT_COLS[p])], rs[p].at[place],
            sum_r.at[p, place], sibling)

    def keep(p, place):
        rows = hidden_rows(p, place)
        swaps[p, place].wait_recv()
        for c, size in pieces(p):
            piece = jnp.dot(rows, wd[core, :, pl.ds(OFFSET[p] + c, size)], preferred_element_type=F32)
            theirs = rs[p][place, :, :, :, pl.ds(c, size)].reshape(256, size).astype(F32)
            os[p][place, :, :, :, pl.ds(c, size)] = (piece + theirs).astype(BF).reshape(4, 4, ROWS, size)

    def add(ref, *more):
        total = ref[...].astype(F32)
        for one in more:
            total = total + one[...].astype(F32)
        ref[...] = total.astype(BF)

    def sum_view(p, k, place, c, part=None):
        prefix = {0: (0, 0, place), 1: (0, place), 2: (place,)}[k]
        return os[p].at[(*prefix, *cut(chunks_of(k)[c], part, OUT_COLS[p]))]

    def passing_view(p, k, c, part=None):
        return passing[k, p].at[cut(chunks_of(k)[c], part, OUT_COLS[p])]

    def side_view(p, k, n, c, part=None):
        return sides[k, p].at[(n, *cut(chunks_of(k)[c], part, OUT_COLS[p]))]

    def rs_slot(k, c, n):
        return (13, 10, 0)[k] + (2 if k == 2 else 1) * c + n

    def toss(p, k, c, n, src, dst, to):
        send(src, dst, rs_r.at[p, rs_slot(k, c, n)], to[ORDER[p][k]])

    def toss_far(p, k, c):
        toss(p, k, c, 0, sum_view(p, k, FAR, c, A), passing_view(p, k, c, A), right)
        toss(p, k, c, 0, sum_view(p, k, FAR, c, B), passing_view(p, k, c, B), left)

    def toss_right(p, k, c):
        toss(p, k, c, 1, sum_view(p, k, RIGHT, c, B), side_view(p, k, 0, c, B), right)

    def toss_left(p, k, c):
        toss(p, k, c, 1, sum_view(p, k, LEFT, c, A), side_view(p, k, 1, c, A), left)

    def pass_on(p, k, c):
        landed(passing_view(p, k, c), rs_r.at[p, rs_slot(k, c, 0)])
        add(sum_view(p, k, RIGHT, c, A), passing_view(p, k, c, A))
        toss(p, k, c, 1, sum_view(p, k, RIGHT, c, A), side_view(p, k, 0, c, A), right)
        add(sum_view(p, k, LEFT, c, B), passing_view(p, k, c, B))
        toss(p, k, c, 1, sum_view(p, k, LEFT, c, B), side_view(p, k, 1, c, B), left)

    def complete(p, k, c):
        landed(side_view(p, k, slice(None), c), rs_r.at[p, rs_slot(k, c, 1)])
        add(sum_view(p, k, OWN, c), side_view(p, k, 0, c), side_view(p, k, 1, c))

    def straight(p, k):
        for n, place, to in ((0, RIGHT, right), (1, LEFT, left), (2, FAR, far)):
            toss(p, k, 0, 0, sum_view(p, k, place, 0), threes[k, p].at[n], to)

    def straight_done(p, k):
        landed(threes[k, p], rs_r.at[p, rs_slot(k, 0, 0)])
        return [threes[k, p][n] for n in range(3)]

    actions = {FAR: toss_far, RIGHT: toss_right, LEFT: toss_left}

    def produce(tasks, following):
        for n, (p, place) in enumerate(tasks):
            ahead = tasks[n + 1] if n + 1 < len(tasks) else following
            if ahead:
                give(*ahead)
            keep(p, place)
            if place in actions:
                for c in (4, 3, 1, 2, 0):
                    actions[place](p, 2, c)

    tasks = [(p, place) for place in (FAR, RIGHT, LEFT) for p in PARTS]
    give(*tasks[0])
    produce(tasks, (0, OWN))
    for p in PARTS:
        pass_on(p, 2, 4)
    for p in PARTS:
        pass_on(p, 2, 3)
    produce([(p, OWN) for p in PARTS], None)
    for p in PARTS:
        pass_on(p, 2, 1)
    for p in PARTS:
        complete(p, 2, 4)
        toss_far(p, 1, 1)
    for p in PARTS:
        pass_on(p, 2, 2)
        pass_on(p, 2, 0)
    for p in PARTS:
        complete(p, 2, 3)
        toss_right(p, 1, 1)
        toss_left(p, 1, 1)
    for p in PARTS:
        complete(p, 2, 1)
        pass_on(p, 1, 1)
    for p in PARTS:
        complete(p, 2, 2)
        straight(p, 1)
    for p in PARTS:
        complete(p, 1, 1)
        straight(p, 0)
    for p in PARTS:
        complete(p, 2, 0)
    here = []
    for p in PARTS:
        total = os[p][0, 0, 0].astype(F32)
        for one in straight_done(p, 1) + straight_done(p, 0):
            total = total + one.astype(F32)
        low, up = total[0:8], total[8:16]
        here.append(jnp.where(core == 0, low, up))
        fin_out[:, pl.ds(OFFSET[p], OUT_COLS[p])] = jnp.where(core == 0, up, low)
    last = send(fin_out, fin_in, end_r.at[1], sibling)
    for p in PARTS:
        at = pl.ds(pl.multiple_of(core * HALF + OFFSET[p], 128), OUT_COLS[p])
        out[:, at] = (tokens[:, at].astype(F32) + here[p]).astype(BF)
    last.wait_recv()
    at = pl.ds(pl.multiple_of(other * HALF, 128), HALF)
    out[:, at] = (tokens[:, at].astype(F32) + fin_in[...]).astype(BF)
    settle()
    pltpu.make_async_copy(packed.at[pl.ds(0, 31)], dbuf.at[pl.ds(0, 31)], d_s).wait()


def fused(tokens, routes, weights, packed, expert_gate, expert_up, expert_down):
    vmem = pl.BlockSpec(memory_space=pltpu.VMEM)
    hbm = pl.BlockSpec(memory_space=pl.ANY)
    cube = (4, 4, 4, ROWS)
    scratch = [pltpu.VMEM((2, *cube, IN_COLS[p]), BF) for p in PARTS]
    scratch += [pltpu.VMEM((*cube, OUT_COLS[p]), BF) for p in PARTS] * 2
    scratch += [pltpu.VMEM((*(4,) * k, ROWS, OUT_COLS[p]), BF) for k in (1, 2) for p in PARTS]
    scratch += [pltpu.VMEM((2, *(4,) * k, ROWS, OUT_COLS[p]), BF) for k in (1, 2) for p in PARTS]
    scratch += [pltpu.VMEM((3, ROWS, OUT_COLS[p]), BF) for k in (0, 1) for p in PARTS]
    scratch += [
        pltpu.VMEM((3, EXPERT_ROWS, WIDTH), BF),
        pltpu.VMEM((2, UNITS, HALF), BF),
        pltpu.VMEM((2, UNITS, HALF), BF),
        pltpu.VMEM((2, UNITS, HALF), BF),
        pltpu.VMEM((*cube, UNITS), F32),
        pltpu.VMEM((*cube, UNITS), F32),
        pltpu.VMEM((*cube, UNITS), BF),
        pltpu.VMEM((8, HALF + 128), F32),
        pltpu.VMEM((8, HALF + 128), F32),
        pltpu.VMEM((8, HALF), F32),
        pltpu.VMEM((8, HALF), F32),
        pltpu.VMEM((32, 64, 256), BF),
        pltpu.SemaphoreType.DMA((3,)),
        pltpu.SemaphoreType.DMA,
        pltpu.SemaphoreType.DMA,
        pltpu.SemaphoreType.DMA((FLIGHTS,)),
        pltpu.SemaphoreType.DMA((3, 15)),
        pltpu.SemaphoreType.DMA((3, 5)),
        pltpu.SemaphoreType.DMA((3, 14)),
        pltpu.SemaphoreType.DMA((3, 4)),
        pltpu.SemaphoreType.DMA((2,)),
    ]
    return pl.pallas_call(
        kernel,
        out_shape=jax.ShapeDtypeStruct((8, WIDTH), BF),
        in_specs=[vmem, vmem, vmem, hbm, hbm, hbm, hbm],
        out_specs=vmem,
        scratch_shapes=scratch,
        cost_estimate=pl.CostEstimate(flops=2 * 1024 * 192 * 7168 * 3, bytes_accessed=8_000_000, transcendentals=1024 * 192),
        compiler_params=pltpu.CompilerParams(
            collective_id=0, has_side_effects=True, vmem_limit_bytes=63 * 2**20),
    )(tokens, routes, weights, packed, expert_gate, expert_up, expert_down)


def per_device(tokens, routes, gate_weights, dense_gate, dense_up, dense_down, expert_gate, expert_up, expert_down):
    mains, tails = [], []
    for weight in (dense_gate, dense_up, dense_down):
        turned = weight.T
        mains.append(turned[:512].reshape(32, 16, DEPTH))
        tails.append(turned[512:].reshape(32, 4, DEPTH))
    tails.append(jnp.zeros((32, 4, DEPTH), BF))
    packed = jnp.pad(jnp.concatenate(mains + tails, axis=1), ((0, 0), (0, 0), (0, 256 - DEPTH)))
    return fused(tokens, routes.T, gate_weights.T, packed, expert_gate, expert_up, expert_down)


def solution(mesh):
    return jax.shard_map(
        per_device,
        mesh=mesh,
        in_specs=(
            P(("ep", "tp"), None),
            P(("ep", "tp"), None),
            P(("ep", "tp"), None),
            P("ep", "tp"),
            P("ep", "tp"),
            P("ep", "tp"),
            P("tp", "ep", None),
            P("tp", "ep", None),
            P("tp", "ep", None),
        ),
        out_specs=P(("ep", "tp"), None),
        check_vma=False,
    )
```

time: 954 us -> 108 us (0.11)
  waiting for transfers between devices: 814 us -> 0 us
  Pallas kernels: 0 us -> 100 us
  matrix products: 51.4 us -> 0 us
  blocking collectives: 45.2 us -> 0 us
  starting transfers between devices: 24 us -> 0 us
  between operations: 13.6 us -> 0.12 us
    all_gather x4 -> x0, waiting for transfers between devices: 601 us -> none  [the longest x1 170 us: per_device(): lax.all_gather(dense_down, 'ep', axis=0, tiled=True)]
    reduce_scatter x2 -> x0, waiting for transfers between devices: 201 us -> none  [the longest x1 187 us: per_device(): lax.psum_scatter(jnp.dot(hidden_all, local_down, preferred_element_type=j...]
    pallas_call x0 -> x1, Pallas kernels: none -> 100 us  [fused(): pl.pallas_call(kernel, out_shape=jax.ShapeDtypeStruct((8, WIDTH), BF), in...]
    dot_general x5 -> x0, matrix products: 51.4 us -> none  [the longest x1 22.9 us: per_device(): jnp.dot(hidden_all, local_down, preferred_element_type=jnp.float32)]
    all_gather x1 -> x0, blocking collectives: 30.4 us -> none  [per_device(): gathered = lax.all_gather(tokens, 'tp', axis=0, tiled=True)]
    all_to_all x1 -> x0, starting transfers between devices: 23.8 us -> none  [per_device(): lax.all_to_all(computed, 'tp', split_axis=0, concat_axis=0, tiled=True)]
    all_to_all x1 -> x0, blocking collectives: 14.8 us -> none  [per_device(): lax.all_to_all(outgoing, 'tp', split_axis=0, concat_axis=0, tiled=True)]
  transfers between devices with their start and end apart: 7 -> 0, of which waited for: 7 -> 0; matrix products, arithmetic and copies ran while one was open for 5% -> 0% of each run, Pallas kernels for 0% -> 0%
where the time goes in v2:
time: 108 us
  Pallas kernels  100 us (93%)
  local copies, waits for them, and re-layouts  7.56 us (7%)
    pallas_call x1, Pallas kernels, fused(): pl.pallas_call(kernel, out_shape=jax.ShapeDtypeStruct((8, WIDTH), BF), in...  100 us
    slice x6, local copies, waits for them, and re-layouts, per_device(): tails.append(turned[512:].reshape(32, 4, DEPTH))  2.85 us

profile of v2, /device:TPU:1, one launch (start us, length us, event | category | flops | bytes accessed | tf_op | source)
XLA Modules:
  0.0 108.1 jit_solution(2580189061478205848)
XLA Ops:
  0.0 0.0 copy-start.1
  0.0 0.0 copy-start
  0.0 0.9 slice.27
  0.9 0.1 copy.19
  1.0 0.8 slice.28
  1.9 0.1 copy.20
  2.0 0.8 slice.29
  2.8 0.1 copy.21
  3.0 1.0 slice.24
  3.9 0.1 copy.16
  4.1 0.0 copy-done
  4.1 0.1 copy.17
  4.3 0.0 copy-done.1
  4.3 0.1 copy.18
  4.5 0.5 concatenate.3
  4.9 1.2 %pad.4.packed = bf16[32,64,256]{2,1,0:T(8,128)(2,1)} pad(bf16[32,64,224]{2,1,0:T(8,128)(2,1)S(1)} %concatenate.3, bf16[]{:T(256)} %constant.1.clone.1), padding=0_0x0_0x0_32 | pad | bytes 1966082 | tf_op jit(solution)/shard_map/jit(_pad)/pad | solution.py:504
  6.1 100.4 %shard_map.91 = bf16[8,7168]{1,0:T(8,128)(2,1)} custom-call(bf16[8,7168]{1,0:T(8,128)(2,1)} %tokens.1, s32[2,8]{1,0:T(2,128)} %bitcast.17, f32[2,8]{1,0:T(2,128)} %bitcast.18, bf16[32,64,256]{2,1,0:T(8,128)(2,1)} %pad.4.packed, bf16[1,152,7168]{2,1,0:T(8,128)(2,1)} %expert_gate.1, bf16[1,152,7168]{2,1,0:T(8,128)(2,1)} %expert_up.1, ...), custom_call_target="tpu_custom_call" | custom-call | flops 8455716864 | bytes 8000000 | tf_op jit(solution)/shard_map/pallas_call | solution.py:485
  106.5 1.6 %copy.23 = bf16[8,7168]{1,0:T(8,128)(2,1)} copy(bf16[8,7168]{1,0:T(8,128)(2,1)} %shard_map.91) | data formatting | bytes 229376
  (6 shorter events, 0.1 us)
Async XLA Ops:
  0.0 4.3 %copy-start.1 = (bf16[224,640]{1,0:T(8,128)(2,1)S(1)}, bf16[224,640]{1,0:T(8,128)(2,1)}, u32[]{:S(2)}) copy-start(bf16[224,640]{1,0:T(8,128)(2,1)} %param.14) | copy-start | bytes 860164
  0.0 4.1 %copy-start = (bf16[224,640]{1,0:T(8,128)(2,1)S(1)}, bf16[224,640]{1,0:T(8,128)(2,1)}, u32[]{:S(2)}) copy-start(bf16[224,640]{1,0:T(8,128)(2,1)} %param.13) | copy-start | bytes 860164

commit v3 on v2

--- a/solution.py
+++ b/solution.py
@@ -46,7 +46,7 @@
 
 
 def kernel(
-    tokens, routes, weights, packed, expert_gate, expert_up, expert_down,
+    tokens, routes, weights, dense_gate, dense_up, dense_down, expert_gate, expert_up, expert_down,
     out,
     x0, x1, x2, o0, o1, o2, r0, r1, r2,
     *rest,
@@ -56,7 +56,7 @@
     sides = {(k, p): rest[6 + (k - 1) * 3 + p] for k in (1, 2) for p in PARTS}
     threes = {(k, p): rest[12 + k * 3 + p] for k in (0, 1) for p in PARTS}
     rest = rest[18:]
-    (raw, wg, wu, wd, ga, ua, hid, tok_out, tok_in, fin_out, fin_in, dbuf,
+    (raw, wg, wu, wd, ga, ua, hid, tok_out, tok_in, fin_out, fin_in, packed, dbuf,
      w_sem, d_s, d_r, out_s, ag_r, sib_r, rs_r, sum_r, end_r) = rest
 
     ep, tp = lax.axis_index("ep"), lax.axis_index("tp")
@@ -85,7 +85,6 @@
         pltpu.make_async_copy(w.at[0], raw.at[n], w_sem.at[n])
         for n, w in enumerate((expert_gate, expert_up, expert_down))
     ]
-    loads.append(pltpu.make_async_copy(packed.at[ep], dbuf.at[ep], d_r))
     for load in loads:
         load.start()
 
@@ -204,6 +203,22 @@
                     n = (i * 4 + j) * ROWS
                     acc[where(p, place, i, j)] += piece[n:n + ROWS]
 
+    def dense_pack():
+        tails = []
+        for n, w in enumerate((dense_gate, dense_up, dense_down)):
+            rows = jnp.concatenate([w[...].astype(F32), jnp.zeros((256 - DEPTH, 640), F32)], axis=0)
+            turned = rows.T.astype(BF)
+            packed[:, pl.ds(16 * n, 16), :] = turned[:512].reshape(32, 16, 256)
+            tails.append(turned[512:])
+        place = lax.broadcasted_iota(jnp.int32, (512, 384), 0)
+        unit = lax.broadcasted_iota(jnp.int32, (512, 384), 1)
+        to, row = lax.div(place, 16), lax.rem(place, 16)
+        wanted = lax.div(row, 4) * 128 + to * 4 + lax.rem(row, 4)
+        pick = jnp.where(unit == wanted, 1.0, 0.0).astype(BF)
+        moved_rows = jnp.dot(pick, jnp.concatenate(tails, axis=0), preferred_element_type=F32)
+        packed[:, pl.ds(48, 16), :] = moved_rows.astype(BF).reshape(32, 16, 256)
+        pltpu.make_async_copy(packed.at[ep], dbuf.at[ep], d_r).start()
+
     def dense_out(first, last):
         for to in peers[first:last]:
             pltpu.make_async_remote_copy(
@@ -236,10 +251,10 @@
         spread(p, 0, direct=True)
     for p in PARTS:
         spread(p, 1, 0, direct=True)
-    dense_out(0, 8)
     for p in PARTS:
         spread(p, 2, 0)
-    dense_out(8, 16)
+    dense_pack()
+    dense_out(0, 16)
     for p in PARTS:
         near(p, 0)
         spread(p, 1, 1)
@@ -450,7 +465,7 @@
     pltpu.make_async_copy(packed.at[pl.ds(0, 31)], dbuf.at[pl.ds(0, 31)], d_s).wait()
 
 
-def fused(tokens, routes, weights, packed, expert_gate, expert_up, expert_down):
+def fused(tokens, routes, weights, dense_gate, dense_up, dense_down, expert_gate, expert_up, expert_down):
     vmem = pl.BlockSpec(memory_space=pltpu.VMEM)
     hbm = pl.BlockSpec(memory_space=pl.ANY)
     cube = (4, 4, 4, ROWS)
@@ -472,6 +487,7 @@
         pltpu.VMEM((8, HALF), F32),
         pltpu.VMEM((8, HALF), F32),
         pltpu.VMEM((32, 64, 256), BF),
+        pltpu.VMEM((32, 64, 256), BF),
         pltpu.SemaphoreType.DMA((3,)),
         pltpu.SemaphoreType.DMA,
         pltpu.SemaphoreType.DMA,
@@ -485,24 +501,18 @@
     return pl.pallas_call(
         kernel,
         out_shape=jax.ShapeDtypeStruct((8, WIDTH), BF),
-        in_specs=[vmem, vmem, vmem, hbm, hbm, hbm, hbm],
+        in_specs=[vmem] * 6 + [hbm] * 3,
         out_specs=vmem,
         scratch_shapes=scratch,
         cost_estimate=pl.CostEstimate(flops=2 * 1024 * 192 * 7168 * 3, bytes_accessed=8_000_000, transcendentals=1024 * 192),
         compiler_params=pltpu.CompilerParams(
             collective_id=0, has_side_effects=True, vmem_limit_bytes=63 * 2**20),
-    )(tokens, routes, weights, packed, expert_gate, expert_up, expert_down)
+    )(tokens, routes, weights, dense_gate, dense_up, dense_down, expert_gate, expert_up, expert_down)
 
 
 def per_device(tokens, routes, gate_weights, dense_gate, dense_up, dense_down, expert_gate, expert_up, expert_down):
-    mains, tails = [], []
-    for weight in (dense_gate, dense_up, dense_down):
-        turned = weight.T
-        mains.append(turned[:512].reshape(32, 16, DEPTH))
-        tails.append(turned[512:].reshape(32, 4, DEPTH))
-    tails.append(jnp.zeros((32, 4, DEPTH), BF))
-    packed = jnp.pad(jnp.concatenate(mains + tails, axis=1), ((0, 0), (0, 0), (0, 256 - DEPTH)))
-    return fused(tokens, routes.T, gate_weights.T, packed, expert_gate, expert_up, expert_down)
+    return fused(
+        tokens, routes.T, gate_weights.T, dense_gate, dense_up, dense_down, expert_gate, expert_up, expert_down)
 
 
 def solution(mesh):

time: 108 us -> 102 us (0.944)
  local copies, waits for them, and re-layouts: 7.56 us -> 1.55 us
    slice x12 -> x0, local copies, waits for them, and re-layouts: 4.24 us -> none  [the longest x6 2.85 us: per_device(): tails.append(turned[512:].reshape(32, 4, DEPTH))]
    pad x1 -> x0, local copies, waits for them, and re-layouts: 1.2 us -> none  [per_device(): jnp.pad(jnp.concatenate(mains + tails, axis=1), ((0, 0), (0, 0), (0, 256...]
where the time goes in v3:
time: 102 us
  Pallas kernels  100 us (98%)
  local copies, waits for them, and re-layouts  1.55 us (2%)
    pallas_call x1, Pallas kernels, fused(): pl.pallas_call(kernel, out_shape=jax.ShapeDtypeStruct((8, WIDTH), BF), in...  100 us

profile of v3, /device:TPU:1, one launch (start us, length us, event | category | flops | bytes accessed | tf_op | source)
XLA Modules:
  0.0 101.9 jit_solution(3420634260017151244)
XLA Ops:
  0.0 100.3 %shard_map.91 = bf16[8,7168]{1,0:T(8,128)(2,1)} custom-call(bf16[8,7168]{1,0:T(8,128)(2,1)} %tokens.1, s32[2,8]{1,0:T(2,128)} %bitcast.2, f32[2,8]{1,0:T(2,128)} %bitcast.3, bf16[224,640]{1,0:T(8,128)(2,1)} %dense_gate.1, bf16[224,640]{1,0:T(8,128)(2,1)} %dense_up.1, bf16[224,640]{1,0:T(8,128)(2,1)} %dense_down.1, bf16[1,152,7168]{2,1,0:T(8,128)(2,1)} %expert_gate.1, ...), custom_call_target="tpu_custom_call" | custom-call | flops 8455716864 | bytes 8000000 | tf_op jit(solution)/shard_map/pallas_call | solution.py:501
  100.4 1.6 %copy.11 = bf16[8,7168]{1,0:T(8,128)(2,1)} copy(bf16[8,7168]{1,0:T(8,128)(2,1)} %shard_map.91) | data formatting | bytes 229376

commit v4 on v3

--- a/solution.py
+++ b/solution.py
@@ -29,14 +29,13 @@
 LINE = (0, OTHERS)
 PLANE = ((0, 0), (0, OTHERS), (OTHERS, 0), (BOTH, OTHERS), (3, OTHERS))
 A, B = 0, 1
+LEAD = 3
 FLIGHTS = 48
 
 
 def cut(selected, part, cols):
     if part is None:
         return tuple(selected)
-    if selected and selected[0] is BOTH:
-        return (1 + part, *selected[1:])
     side = pl.ds(0, CUT) if part == A else pl.ds(CUT, cols - CUT)
     return (*selected, slice(None), side)
 
@@ -257,7 +256,7 @@
     dense_out(0, 16)
     for p in PARTS:
         near(p, 0)
-        spread(p, 1, 1)
+        spread(p, 1, 1, direct=True)
         spread(p, 2, 1)
     dense_out(16, 24)
     for p in PARTS:
@@ -268,7 +267,7 @@
     for p in PARTS:
         relay(p, 2, 0)
     for p in PARTS:
-        relay(p, 1, 1)
+        near(p, 1, 1)
         spread(p, 2, 3)
     for p in PARTS:
         distant(p, 1, 1)
@@ -330,24 +329,26 @@
     def hidden_rows(p, place):
         return jnp.concatenate([hid[where(p, place, i, j)] for i in range(4) for j in range(4)], axis=0)
 
-    def pieces(p):
-        return [(c, min(256, OUT_COLS[p] - c)) for c in range(0, OUT_COLS[p], 256)]
+    def pieces(p, part):
+        start, stop = (0, CUT) if part == A else (CUT, OUT_COLS[p])
+        return start, stop - start, [(c, min(256, stop - c)) for c in range(start, stop, 256)]
 
     swaps = {}
 
-    def give(p, place):
+    def give(p, place, part):
         rows = hidden_rows(p, place)
-        for c, size in pieces(p):
+        start, width, cuts = pieces(p, part)
+        for c, size in cuts:
             piece = jnp.dot(rows, wd[other, :, pl.ds(OFFSET[p] + c, size)], preferred_element_type=F32)
             xs[p][0, place, :, :, :, pl.ds(c, size)] = piece.astype(BF).reshape(4, 4, ROWS, size)
-        swaps[p, place] = send(
-            xs[p].at[0, place, :, :, :, pl.ds(0, OUT_COLS[p])], rs[p].at[place],
-            sum_r.at[p, place], sibling)
-
-    def keep(p, place):
+        swaps[p, place, part] = send(
+            xs[p].at[0, place, :, :, :, pl.ds(start, width)], rs[p].at[place, :, :, :, pl.ds(start, width)],
+            sum_r.at[p, 2 * place + part], sibling)
+
+    def keep(p, place, part):
         rows = hidden_rows(p, place)
-        swaps[p, place].wait_recv()
-        for c, size in pieces(p):
+        swaps[p, place, part].wait_recv()
+        for c, size in pieces(p, part)[2]:
             piece = jnp.dot(rows, wd[core, :, pl.ds(OFFSET[p] + c, size)], preferred_element_type=F32)
             theirs = rs[p][place, :, :, :, pl.ds(c, size)].reshape(256, size).astype(F32)
             os[p][place, :, :, :, pl.ds(c, size)] = (piece + theirs).astype(BF).reshape(4, 4, ROWS, size)
@@ -374,9 +375,12 @@
     def toss(p, k, c, n, src, dst, to):
         send(src, dst, rs_r.at[p, rs_slot(k, c, n)], to[ORDER[p][k]])
 
+    def toss_far_half(p, k, c, part):
+        toss(p, k, c, 0, sum_view(p, k, FAR, c, part), passing_view(p, k, c, part), (right, left)[part])
+
     def toss_far(p, k, c):
-        toss(p, k, c, 0, sum_view(p, k, FAR, c, A), passing_view(p, k, c, A), right)
-        toss(p, k, c, 0, sum_view(p, k, FAR, c, B), passing_view(p, k, c, B), left)
+        toss_far_half(p, k, c, A)
+        toss_far_half(p, k, c, B)
 
     def toss_right(p, k, c):
         toss(p, k, c, 1, sum_view(p, k, RIGHT, c, B), side_view(p, k, 0, c, B), right)
@@ -403,26 +407,34 @@
         landed(threes[k, p], rs_r.at[p, rs_slot(k, 0, 0)])
         return [threes[k, p][n] for n in range(3)]
 
-    actions = {FAR: toss_far, RIGHT: toss_right, LEFT: toss_left}
+    actions = {
+        (FAR, A): lambda p, k, c: toss_far_half(p, k, c, A),
+        (FAR, B): lambda p, k, c: toss_far_half(p, k, c, B),
+        (RIGHT, B): toss_right,
+        (LEFT, A): toss_left,
+    }
 
     def produce(tasks, following):
-        for n, (p, place) in enumerate(tasks):
-            ahead = tasks[n + 1] if n + 1 < len(tasks) else following
+        for n, task in enumerate(tasks):
+            ahead = (tasks + following)[n + LEAD:n + LEAD + 1]
             if ahead:
-                give(*ahead)
-            keep(p, place)
-            if place in actions:
+                give(*ahead[0])
+            keep(*task)
+            action = actions.get(task[1:])
+            if action:
                 for c in (4, 3, 1, 2, 0):
-                    actions[place](p, 2, c)
-
-    tasks = [(p, place) for place in (FAR, RIGHT, LEFT) for p in PARTS]
-    give(*tasks[0])
-    produce(tasks, (0, OWN))
+                    action(task[0], 2, c)
+
+    tasks = [(p, *half) for half in ((FAR, A), (FAR, B), (RIGHT, B), (LEFT, A), (RIGHT, A), (LEFT, B)) for p in PARTS]
+    own_tasks = [(p, OWN, part) for part in (A, B) for p in PARTS]
+    for n in range(LEAD):
+        give(*tasks[n])
+    produce(tasks, own_tasks[:LEAD])
     for p in PARTS:
         pass_on(p, 2, 4)
     for p in PARTS:
         pass_on(p, 2, 3)
-    produce([(p, OWN) for p in PARTS], None)
+    produce(own_tasks, [])
     for p in PARTS:
         pass_on(p, 2, 1)
     for p in PARTS:
@@ -495,7 +507,7 @@
         pltpu.SemaphoreType.DMA((3, 15)),
         pltpu.SemaphoreType.DMA((3, 5)),
         pltpu.SemaphoreType.DMA((3, 14)),
-        pltpu.SemaphoreType.DMA((3, 4)),
+        pltpu.SemaphoreType.DMA((3, 8)),
         pltpu.SemaphoreType.DMA((2,)),
     ]
     return pl.pallas_call(

time: 102 us -> 99.6 us (0.976)
  Pallas kernels: 100 us -> 97.9 us
    pallas_call x1, Pallas kernels: 100 us -> 97.9 us  [fused(): pl.pallas_call(kernel, out_shape=jax.ShapeDtypeStruct((8, WIDTH), BF), in...]
where the time goes in v4:
time: 99.6 us; the launch traced here: 99.4 us
  Pallas kernels  97.9 us (98%)
  local copies, waits for them, and re-layouts  1.55 us (2%)
    pallas_call x1, Pallas kernels, fused(): pl.pallas_call(kernel, out_shape=jax.ShapeDtypeStruct((8, WIDTH), BF), in...  97.9 us

profile of v4, /device:TPU:1, one launch (start us, length us, event | category | flops | bytes accessed | tf_op | source)
XLA Modules:
  0.0 99.4 jit_solution(10792704115037151800)
XLA Ops:
  0.0 97.9 %shard_map.91 = bf16[8,7168]{1,0:T(8,128)(2,1)} custom-call(bf16[8,7168]{1,0:T(8,128)(2,1)} %tokens.1, s32[2,8]{1,0:T(2,128)} %bitcast.2, f32[2,8]{1,0:T(2,128)} %bitcast.3, bf16[224,640]{1,0:T(8,128)(2,1)} %dense_gate.1, bf16[224,640]{1,0:T(8,128)(2,1)} %dense_up.1, bf16[224,640]{1,0:T(8,128)(2,1)} %dense_down.1, bf16[1,152,7168]{2,1,0:T(8,128)(2,1)} %expert_gate.1, ...), custom_call_target="tpu_custom_call" | custom-call | flops 8455716864 | bytes 8000000 | tf_op jit(solution)/shard_map/pallas_call | solution.py:513
  97.9 1.6 %copy.11 = bf16[8,7168]{1,0:T(8,128)(2,1)} copy(bf16[8,7168]{1,0:T(8,128)(2,1)} %shard_map.91) | data formatting | bytes 229376

commit v5 on v4

--- a/solution.py
+++ b/solution.py
@@ -203,19 +203,25 @@
                     acc[where(p, place, i, j)] += piece[n:n + ROWS]
 
     def dense_pack():
-        tails = []
+        tails, later = [], []
         for n, w in enumerate((dense_gate, dense_up, dense_down)):
             rows = jnp.concatenate([w[...].astype(F32), jnp.zeros((256 - DEPTH, 640), F32)], axis=0)
-            turned = rows.T.astype(BF)
-            packed[:, pl.ds(16 * n, 16), :] = turned[:512].reshape(32, 16, 256)
-            tails.append(turned[512:])
+            turned = rows.T
+            packed[:, pl.ds(16 * n, 16), :] = turned[:512, :128].astype(BF).reshape(32, 16, 128)
+            later.append(turned[:512, 128:])
+            tails.append(turned[512:].astype(BF))
         place = lax.broadcasted_iota(jnp.int32, (512, 384), 0)
         unit = lax.broadcasted_iota(jnp.int32, (512, 384), 1)
         to, row = lax.div(place, 16), lax.rem(place, 16)
         wanted = lax.div(row, 4) * 128 + to * 4 + lax.rem(row, 4)
         pick = jnp.where(unit == wanted, 1.0, 0.0).astype(BF)
         moved_rows = jnp.dot(pick, jnp.concatenate(tails, axis=0), preferred_element_type=F32)
-        packed[:, pl.ds(48, 16), :] = moved_rows.astype(BF).reshape(32, 16, 256)
+        packed[:, pl.ds(48, 16), :] = moved_rows[:, :128].astype(BF).reshape(32, 16, 128)
+        spare = lax.broadcasted_iota(jnp.int32, (512, 128), 1) >= 96
+        for n in range(3):
+            ridden = pltpu.roll(moved_rows[:, 128:], 96 - 32 * n, 1)
+            both = jnp.where(spare, ridden, later[n])
+            packed[:, pl.ds(64 + 16 * n, 16), :] = both.astype(BF).reshape(32, 16, 128)
         pltpu.make_async_copy(packed.at[ep], dbuf.at[ep], d_r).start()
 
     def dense_out(first, last):
@@ -224,12 +230,21 @@
                 src_ref=packed.at[to], dst_ref=dbuf.at[ep], send_sem=d_s, recv_sem=d_r,
                 device_id={"ep": to, "tp": tp}, device_id_type=MESH).start()
 
+    def unpacked(source):
+        block = dbuf[source].astype(F32)
+        lanes = lax.div(lax.broadcasted_iota(jnp.int32, (16, 128), 1), 32)
+        tail = jnp.zeros((16, 128), F32)
+        for n in range(3):
+            ridden = pltpu.roll(block[64 + 16 * n:80 + 16 * n], (32 + 32 * n) % 128, 1)
+            tail = jnp.where(lanes == n, ridden, tail)
+        return jnp.concatenate([block[0:64], jnp.concatenate([block[64:112], tail], axis=0)], axis=1)
+
     def dense_in():
         landed(dbuf, d_r)
         row = lax.broadcasted_iota(jnp.int32, (ROWS, RUN), 0)
         for i in range(8):
             at = pl.ds((i % 4) * RUN, RUN)
-            run = jnp.concatenate([dbuf[4 * i + z][:, 0:DEPTH].astype(F32) for z in range(4)], axis=1)
+            run = jnp.concatenate([unpacked(4 * i + z)[:, 0:DEPTH] for z in range(4)], axis=1)
             tail = run[48:64]
             for n, w in enumerate((wg, wu, wd)):
                 w[i // 4, pl.ds(0, 16), at] = run[16 * n:16 * n + 16].astype(BF)
@@ -498,8 +513,8 @@
         pltpu.VMEM((8, HALF + 128), F32),
         pltpu.VMEM((8, HALF), F32),
         pltpu.VMEM((8, HALF), F32),
-        pltpu.VMEM((32, 64, 256), BF),
-        pltpu.VMEM((32, 64, 256), BF),
+        pltpu.VMEM((32, 112, 128), BF),
+        pltpu.VMEM((32, 112, 128), BF),
         pltpu.SemaphoreType.DMA((3,)),
         pltpu.SemaphoreType.DMA,
         pltpu.SemaphoreType.DMA,

time: 99.6 us -> 98.2 us (0.986)
  Pallas kernels: 97.9 us -> 96.5 us
    pallas_call x1, Pallas kernels: 97.9 us -> 96.5 us  [fused(): pl.pallas_call(kernel, out_shape=jax.ShapeDtypeStruct((8, WIDTH), BF), in...]
where the time goes in v5:
time: 98.2 us; the launch traced here: 98 us
  Pallas kernels  96.5 us (98%)
  local copies, waits for them, and re-layouts  1.55 us (2%)
    pallas_call x1, Pallas kernels, fused(): pl.pallas_call(kernel, out_shape=jax.ShapeDtypeStruct((8, WIDTH), BF), in...  96.5 us

profile of v5, /device:TPU:1, one launch (start us, length us, event | category | flops | bytes accessed | tf_op | source)
XLA Modules:
  0.0 98.0 jit_solution(2713495847393553797)
XLA Ops:
  0.0 96.5 %shard_map.91 = bf16[8,7168]{1,0:T(8,128)(2,1)} custom-call(bf16[8,7168]{1,0:T(8,128)(2,1)} %tokens.1, s32[2,8]{1,0:T(2,128)} %bitcast.2, f32[2,8]{1,0:T(2,128)} %bitcast.3, bf16[224,640]{1,0:T(8,128)(2,1)} %dense_gate.1, bf16[224,640]{1,0:T(8,128)(2,1)} %dense_up.1, bf16[224,640]{1,0:T(8,128)(2,1)} %dense_down.1, bf16[1,152,7168]{2,1,0:T(8,128)(2,1)} %expert_gate.1, ...), custom_call_target="tpu_custom_call" | custom-call | flops 8455716864 | bytes 8000000 | tf_op jit(solution)/shard_map/pallas_call | solution.py:528
  96.5 1.6 %copy.11 = bf16[8,7168]{1,0:T(8,128)(2,1)} copy(bf16[8,7168]{1,0:T(8,128)(2,1)} %shard_map.91) | data formatting | bytes 229376
